TPU v7x, 256 devices: a whole 4x4x8 slice. The times are simulated.
256 devices in a mesh: blk: 64 (over x, y_hi, z), dp: 4 (over y_lo, core).
Axes of the slice: x: 4, y: 4 (y_hi: 2, y_lo: 2; y = y_hi * 2 + y_lo), z: 8, core: 2. Of those that a mesh axis runs over, the one named last changes fastest.
Arguments:
- tokens: bfloat16 [98304, 5120], P(('blk', 'dp')), may hold values from -6 to 6
- cotangent: bfloat16 [98304, 5120], P(('blk', 'dp')), may hold values from -0.44921875 to 0.44921875
- gate_weight: bfloat16 [8192, 5120], P('blk'), may hold values from -0.078125 to 0.078125
- up_weight: bfloat16 [8192, 5120], P('blk'), may hold values from -0.078125 to 0.078125
- down_weight: bfloat16 [8192, 5120], P('blk'), may hold values from -0.0625 to 0.0625
Outputs:
- gate_grad: bfloat16 [8192, 5120], P(('blk', 'dp'))
- up_grad: bfloat16 [8192, 5120], P(('blk', 'dp'))
- down_grad: bfloat16 [8192, 5120], P(('blk', 'dp'))
All inputs are finite; a program needn't handle non-finite values.
Results may differ from a plain program's by a relative error of at most 0.005.
Values may be sent and summed in bfloat16 or wider, within the bound.
A program may use at most 128 MiB of HBM per device.

v0:
```python
import jax
import jax.numpy as jnp
from jax import lax
from jax.sharding import PartitionSpec as P


def from_behind(shard, axis, by):
    length = lax.axis_size(axis)
    return lax.ppermute(shard, axis, [(i, (i + by) % length) for i in range(length)])


def block_terms(group_tokens, group_cotangent, w_gate, w_up, w_down):
    gate_pre = jnp.dot(group_tokens, w_gate.T, preferred_element_type=jnp.float32)
    up_pre = jnp.dot(group_tokens, w_up.T, preferred_element_type=jnp.float32)
    squash = jax.nn.sigmoid(gate_pre)
    hidden = (gate_pre * squash * up_pre).astype(jnp.bfloat16)
    down_term = jnp.dot(hidden.T, group_cotangent, preferred_element_type=jnp.float32)
    grad_hidden = jnp.dot(group_cotangent, w_down.T, preferred_element_type=jnp.float32)
    grad_gate_pre = (grad_hidden * up_pre * squash * (1.0 + gate_pre * (1.0 - squash))).astype(
        jnp.bfloat16
    )
    grad_up_pre = (grad_hidden * gate_pre * squash).astype(jnp.bfloat16)
    gate_term = jnp.dot(grad_gate_pre.T, group_tokens, preferred_element_type=jnp.float32)
    up_term = jnp.dot(grad_up_pre.T, group_tokens, preferred_element_type=jnp.float32)
    return (gate_term, up_term, down_term)


def per_device(tokens, cotangent, gate_weight, up_weight, down_weight):
    own_gate, own_up, own_down = block_terms(tokens, cotangent, gate_weight, up_weight, down_weight)
    arrived = from_behind((gate_weight, up_weight, down_weight), "blk", 1)
    later_gate, later_up, later_down = block_terms(
        tokens, cotangent, arrived[0], arrived[1], arrived[2]
    )
    returned = from_behind((later_gate, later_up, later_down), "blk", -1)
    cycle_gate = own_gate + returned[0]
    cycle_up = own_up + returned[1]
    cycle_down = own_down + returned[2]
    share_rows = cycle_gate.shape[0] // lax.axis_size("dp")
    summed = lax.psum((cycle_gate, cycle_up, cycle_down), "dp")
    first_row = lax.axis_index("dp") * share_rows
    return tuple(
        (
            lax.dynamic_slice_in_dim(part, first_row, share_rows, 0).astype(jnp.bfloat16)
            for part in summed
        )
    )


def solution(mesh):
    in_specs = (
        P(("blk", "dp"), None),
        P(("blk", "dp"), None),
        P("blk", None),
        P("blk", None),
        P("blk", None),
    )
    out_specs = (P(("blk", "dp"), None), P(("blk", "dp"), None), P(("blk", "dp"), None))
    return jax.shard_map(
        per_device, mesh=mesh, in_specs=in_specs, out_specs=out_specs, check_vma=False
    )
```

profile of v0, /device:TPU:1, one launch (start us, length us, event | category | flops | bytes accessed | tf_op | source)
XLA Modules:
  0.0 416.1 jit_solution(10856191280695803148)
XLA Ops:
  0.6 0.0 copy-start
  0.6 2.5 collective-permute-start.2
  3.2 1.6 collective-permute-start.1
  4.8 1.6 collective-permute-start
  6.5 34.2 %collective-permute-done.2 = bf16[128,5120]{1,0:T(8,128)(2,1)S(1)} collective-permute-done((bf16[128,5120]{1,0:T(8,128)(2,1)}, bf16[128,5120]{1,0:T(8,128)(2,1)S(1)}, u32[]{:S(2)}, u32[]{:S(2)}) %collective-permute-start.2) | collective-permute-done | bytes 1310752 | tf_op jit(solution)/shard_map/ppermute | solution.py:9
  40.7 3.3 fusion.20
  44.0 0.0 copy-start.2
  44.0 24.7 %collective-permute-done.1 = bf16[128,5120]{1,0:T(8,128)(2,1)S(1)} collective-permute-done((bf16[128,5120]{1,0:T(8,128)(2,1)}, bf16[128,5120]{1,0:T(8,128)(2,1)S(1)}, u32[]{:S(2)}, u32[]{:S(2)}) %collective-permute-start.1) | collective-permute-done | bytes 1310752 | tf_op jit(solution)/shard_map/ppermute | solution.py:9
  68.8 0.0 copy-done
  68.8 1.2 fusion.19
  69.9 26.9 %collective-permute-done = bf16[128,5120]{1,0:T(8,128)(2,1)S(1)} collective-permute-done((bf16[128,5120]{1,0:T(8,128)(2,1)}, bf16[128,5120]{1,0:T(8,128)(2,1)S(1)}, u32[]{:S(2)}, u32[]{:S(2)}) %collective-permute-start) | collective-permute-done | bytes 1310752 | tf_op jit(solution)/shard_map/ppermute | solution.py:9
  96.8 0.0 copy-done.2
  96.8 1.2 fusion.18
  98.0 0.9 fusion
  99.0 1.2 collective-permute-start.3
  100.2 2.5 fusion.2
  102.6 0.7 collective-permute-start.5
  103.4 2.5 fusion.1
  105.9 0.7 collective-permute-start.4
  106.6 0.0 copy-start.3
  106.6 0.0 copy-start.4
  106.6 3.8 fusion.17
  110.4 0.0 copy-done.3
  110.4 0.2 copy-done.4
  110.7 0.0 copy-start.1
  110.7 0.0 copy-start.5
  110.7 1.2 fusion.15
  111.9 0.9 copy-done.1
  112.8 0.4 copy-done.5
  113.2 1.2 fusion.16
  114.3 42.0 %collective-permute-done.3 = f32[128,5120]{1,0:T(8,128)} collective-permute-done((f32[128,5120]{1,0:T(8,128)S(1)}, f32[128,5120]{1,0:T(8,128)}, u32[]{:S(2)}, u32[]{:S(2)}) %collective-permute-start.3) | collective-permute-done | bytes 2621472 | tf_op jit(solution)/shard_map/ppermute | solution.py:9
  156.3 4.2 %convolution_add_fusion.2 = f32[128,5120]{1,0:T(8,128)} fusion(f32[128,5120]{1,0:T(8,128)} %collective-permute-done.3, bf16[384,5120]{1,0:T(8,128)(2,1)S(1)} %copy-done.1, f32[384,128]{1,0:T(8,128)S(1)} %fusion.17, f32[384,128]{1,0:T(8,128)S(1)} %fusion.15, f32[384,128]{1,0:T(8,128)S(1)} %fusion.16), kind=kOutput, calls=%fused_computation.2 | convolution fusion | flops 504463360 | bytes 9764864 | tf_op jit(solution)/shard_map/dot_general | solution.py:23
  160.5 52.0 %collective-permute-done.5 = f32[128,5120]{1,0:T(8,128)} collective-permute-done((f32[128,5120]{1,0:T(8,128)}, f32[128,5120]{1,0:T(8,128)}, u32[]{:S(2)}, u32[]{:S(2)}) %collective-permute-start.5) | collective-permute-done | bytes 2621472 | tf_op jit(solution)/shard_map/ppermute | solution.py:9
  212.5 2.7 convolution_add_fusion
  215.2 53.5 %collective-permute-done.4 = f32[128,5120]{1,0:T(8,128)} collective-permute-done((f32[128,5120]{1,0:T(8,128)}, f32[128,5120]{1,0:T(8,128)}, u32[]{:S(2)}, u32[]{:S(2)}) %collective-permute-start.4) | collective-permute-done | bytes 2621472 | tf_op jit(solution)/shard_map/ppermute | solution.py:9
  268.6 4.2 %convolution_add_fusion.1 = f32[128,5120]{1,0:T(8,128)} fusion(f32[128,5120]{1,0:T(8,128)} %collective-permute-done.4, bf16[384,5120]{1,0:T(8,128)(2,1)S(1)} %copy-done.1, f32[384,128]{1,0:T(8,128)S(1)} %fusion.15, f32[384,128]{1,0:T(8,128)S(1)} %fusion.17), kind=kOutput, calls=%fused_computation.1 | convolution fusion | flops 504266752 | bytes 9568256 | tf_op jit(solution)/shard_map/dot_general | solution.py:24
  272.8 139.7 %all-reduce.2 = (bf16[128,5120]{1,0:T(8,128)(2,1)}, bf16[128,5120]{1,0:T(8,128)(2,1)}, bf16[128,5120]{1,0:T(8,128)(2,1)}) all-reduce(f32[128,5120]{1,0:T(8,128)} %convolution_add_fusion.2, f32[128,5120]{1,0:T(8,128)} %convolution_add_fusion.1, f32[128,5120]{1,0:T(8,128)S(1)} %convolution_add_fusion), channel_id=1, replica_groups=mesh['blk'=64,'dp'=4] {'dp'}, use_global_device_ids=true, to_apply=%region_0.0 | all-reduce | flops 1966080 | bytes 11796480 | tf_op jit(solution)/shard_map/psum | solution.py:39
  412.5 1.7 dynamic-slice_convert_fusion.2
  414.2 1.9 dynamic-slice_convert_fusion
Async XLA Ops:
  0.6 68.1 %copy-start = (bf16[384,5120]{1,0:T(8,128)(2,1)S(1)}, bf16[384,5120]{1,0:T(8,128)(2,1)}, u32[]{:S(2)}) copy-start(bf16[384,5120]{1,0:T(8,128)(2,1)} %param.5) | copy-start | bytes 11796484
  0.6 40.0 %collective-permute-start.2 = (bf16[128,5120]{1,0:T(8,128)(2,1)}, bf16[128,5120]{1,0:T(8,128)(2,1)S(1)}, u32[]{:S(2)}, u32[]{:S(2)}) collective-permute-start(bf16[128,5120]{1,0:T(8,128)(2,1)} %param.7), channel_id=1, source_target_pairs={{0,4},{4,8},{8,12},{12,16},{16,20},{20,24},{24,28},{28,32},{32,36}... | collective-permute-start | bytes 3932168 | tf_op jit(solution)/shard_map/ppermute | solution.py:9
  3.2 65.6 %collective-permute-start.1 = (bf16[128,5120]{1,0:T(8,128)(2,1)}, bf16[128,5120]{1,0:T(8,128)(2,1)S(1)}, u32[]{:S(2)}, u32[]{:S(2)}) collective-permute-start(bf16[128,5120]{1,0:T(8,128)(2,1)} %param.8), channel_id=1, source_target_pairs={{0,4},{4,8},{8,12},{12,16},{16,20},{20,24},{24,28},{28,32},{32,36}... | collective-permute-start | bytes 3932168 | tf_op jit(solution)/shard_map/ppermute | solution.py:9
  4.8 92.0 %collective-permute-start = (bf16[128,5120]{1,0:T(8,128)(2,1)}, bf16[128,5120]{1,0:T(8,128)(2,1)S(1)}, u32[]{:S(2)}, u32[]{:S(2)}) collective-permute-start(bf16[128,5120]{1,0:T(8,128)(2,1)} %param.9), channel_id=1, source_target_pairs={{0,4},{4,8},{8,12},{12,16},{16,20},{20,24},{24,28},{28,32},{32,36}... | collective-permute-start | bytes 3932168 | tf_op jit(solution)/shard_map/ppermute | solution.py:9
  44.0 52.8 %copy-start.2 = (bf16[384,5120]{1,0:T(8,128)(2,1)S(1)}, bf16[384,5120]{1,0:T(8,128)(2,1)}, u32[]{:S(2)}) copy-start(bf16[384,5120]{1,0:T(8,128)(2,1)} %param.6) | copy-start | bytes 11796484
  99.0 57.3 %collective-permute-start.3 = (f32[128,5120]{1,0:T(8,128)S(1)}, f32[128,5120]{1,0:T(8,128)}, u32[]{:S(2)}, u32[]{:S(2)}) collective-permute-start(f32[128,5120]{1,0:T(8,128)S(1)} %fusion), channel_id=1, source_target_pairs={{0,252},{4,0},{8,4},{12,8},{16,12},{20,16},{24,20},{28,24},{32,28}... | collective-permute-start | bytes 7864328 | tf_op jit(solution)/shard_map/ppermute | solution.py:9
  102.6 109.8 %collective-permute-start.5 = (f32[128,5120]{1,0:T(8,128)}, f32[128,5120]{1,0:T(8,128)}, u32[]{:S(2)}, u32[]{:S(2)}) collective-permute-start(f32[128,5120]{1,0:T(8,128)} %fusion.2), channel_id=1, source_target_pairs={{0,252},{4,0},{8,4},{12,8},{16,12},{20,16},{24,20},{28,24},{32,28}... | collective-permute-start | bytes 7864328 | tf_op jit(solution)/shard_map/ppermute | solution.py:9
  105.9 162.8 %collective-permute-start.4 = (f32[128,5120]{1,0:T(8,128)}, f32[128,5120]{1,0:T(8,128)}, u32[]{:S(2)}, u32[]{:S(2)}) collective-permute-start(f32[128,5120]{1,0:T(8,128)} %fusion.1), channel_id=1, source_target_pairs={{0,252},{4,0},{8,4},{12,8},{16,12},{20,16},{24,20},{28,24},{32,28}... | collective-permute-start | bytes 7864328 | tf_op jit(solution)/shard_map/ppermute | solution.py:9
  106.6 3.8 copy-start.3
  106.6 4.1 copy-start.4
  110.7 2.1 copy-start.1
  110.7 2.5 copy-start.5
where the time goes:
time: 416 us
  waiting for transfers between devices  233 us (56%)
  blocking collectives  140 us (34%)
  matrix products  28.9 us (7%)
  starting transfers between devices  8.49 us (2%)
  local copies, waits for them, and re-layouts  5.17 us (1%)
    ppermute x6, waiting for transfers between devices, from_behind(): lax.ppermute(shard, axis, [(i, (i + by) % length) for i in range(length)])  233 us
    psum x1, blocking collectives, per_device(): summed = lax.psum((cycle_gate, cycle_up, cycle_down), 'dp')  140 us
    ppermute x6, starting transfers between devices, from_behind(): lax.ppermute(shard, axis, [(i, (i + by) % length) for i in range(length)])  8.49 us
  transfers between devices with their start and end apart: 6, of which 6 were waited for; matrix products, arithmetic and copies ran while one was open for 5% of the time, Pallas kernels for 0%

commit v1 on v0

v1 whole, which is shorter than its diff:
```python
import functools

import jax
import jax.numpy as jnp
from jax import lax
from jax.experimental import pallas as pl
from jax.experimental.pallas import tpu as pltpu
from jax.sharding import PartitionSpec as P

MESH = pl.DeviceIdType.MESH
NT = (((1,), (1,)), ((), ()))
NN = (((1,), (0,)), ((), ()))
Z_LEN = 8
CHUNKS = 4
SUB = 16
RELAY = (0, 1)
DIRECT = (2, 3)
BACK_FIRST = (0, 1)
ACROSS_FIRST = (2, 3)


def dot(a, b, dims):
    return lax.dot_general(a, b, dims, preferred_element_type=jnp.float32)


def f32(v):
    return v.astype(jnp.float32)


def bf16(v):
    return v.astype(jnp.bfloat16)


def kernel(
    n_blk, x_hbm, c_hbm, wg_hbm, wu_hbm, wd_hbm, out_hbm,
    xv, cv, w_own, w_in,
    own_pair_out, own_pair_in, own_sum,
    in_pair_out, in_pair_in, in_sum,
    back_out, back_in, across_in_out, across_in_in, across_out, across_own_in, final,
    load_sem, up_send, up_recv, fwd_send, fwd_recv, relay_send, relay_recv, fwd2_send, fwd2_recv,
    own_pair_send, own_pair_recv, in_pair_send, in_pair_recv,
    back_send, back_recv, across_in_send, across_in_recv, across_send, across_recv, fin_send, fin_recv,
):
    j = lax.axis_index("blk")
    r = lax.axis_index("dp")
    chip = lax.div(r, 2)
    core = lax.rem(r, 2)
    place = lax.rem(j, Z_LEN)
    flip_up = jnp.where(place == Z_LEN - 1, 1, 0)
    flip_down = jnp.where(place == 0, 1, 0)
    up_chip = lax.rem(chip + flip_up, 2)
    down_chip = lax.rem(chip + flip_down, 2)
    up = (lax.rem(j + 1, n_blk), up_chip * 2 + core)
    down = (lax.rem(j + n_blk - 1, n_blk), down_chip * 2 + core)
    across = (j, (1 - chip) * 2 + core)
    sibling = (j, chip * 2 + 1 - core)
    half = xv.shape[1] // 2
    mine = pl.ds(pl.multiple_of(core * half, half), half)
    theirs = pl.ds(pl.multiple_of((1 - core) * half, half), half)
    w_hbm = (wg_hbm, wu_hbm, wd_hbm)

    def remote(src, dst, send, recv, device):
        return pltpu.make_async_remote_copy(
            src_ref=src, dst_ref=dst, send_sem=send, recv_sem=recv, device_id=device, device_id_type=MESH
        )

    loads = []
    for m in range(3):
        for p in range(2):
            loads.append(pltpu.make_async_copy(w_hbm[m].at[p], w_own.at[:, p, m], load_sem.at[m * 2 + p]))
    load_x = pltpu.make_async_copy(x_hbm, xv, load_sem.at[6])
    load_c = pltpu.make_async_copy(c_hbm, cv, load_sem.at[7])
    for load in loads[:4]:
        load.start()
    load_x.start()
    for load in loads[4:]:
        load.start()
    load_c.start()

    barrier = pltpu.get_barrier_semaphore()
    for device in (up, down, across, sibling):
        pl.semaphore_signal(barrier, inc=1, device_id=device, device_id_type=MESH)
    pl.semaphore_wait(barrier, 4)

    pending = []

    def go(copy):
        copy.start()
        pending.append(copy)
        return copy

    up_copies = {}
    for k in RELAY + DIRECT:
        for m in range(3):
            if k in RELAY:
                src, dst = w_hbm[m].at[up_chip, k, :, mine], w_in.at[k, up_chip, m, :, mine]
            else:
                src, dst = w_hbm[m].at[:, k, :, mine], w_in.at[k, :, m, :, mine]
            up_copies[k, m] = go(remote(src, dst, up_send.at[k, m], up_recv.at[k, m], up))

    fwd, relay, fwd2 = {}, {}, {}

    def forward(k):
        for m in range(3):
            up_copies[k, m].wait_recv()
            if k in RELAY:
                piece = w_in.at[k, chip, m, :, mine]
                relay[k, m] = go(remote(piece, piece, relay_send.at[k, m], relay_recv.at[k, m], across))
            else:
                piece = w_in.at[k, :, m, :, mine]
            fwd[k, m] = go(remote(piece, piece, fwd_send.at[k, m], fwd_recv.at[k, m], sibling))

    def forward_relayed(k):
        for m in range(3):
            relay[k, m].wait_recv()
            piece = w_in.at[k, 1 - chip, m, :, mine]
            fwd2[k, m] = go(remote(piece, piece, fwd2_send.at[k, m], fwd2_recv.at[k, m], sibling))

    def arrived(k, m):
        fwd[k, m].wait_recv()
        if k in RELAY:
            fwd2[k, m].wait_recv()

    def project(w, lo, n, rows, act):
        total = None
        for s in (pl.ds(0, half), pl.ds(half, half)):
            part = w[:, :, lo:lo + n, :, s] if len(w.shape) == 5 else w[:, lo:lo + n, :, s]
            term = dot(part.reshape(rows, half), act[:, s], NT)
            total = term if total is None else total + term
        return total

    def hidden_grads(pre, grad_hidden, groups):
        tok = pre.shape[-1]
        pre = pre.reshape(groups, 2, SUB, tok)
        gate, up_pre = pre[:, 0], pre[:, 1]
        grad_hidden = grad_hidden.reshape(groups, SUB, tok)
        squash = jax.nn.sigmoid(gate)
        silu = gate * squash
        hidden = bf16(silu * up_pre)
        gg = bf16(grad_hidden * up_pre * squash * (1.0 + gate * (1.0 - squash)))
        gu = bf16(grad_hidden * silu)
        both = jnp.stack([gg, gu], axis=1).reshape(groups * 2 * SUB, tok)
        return both, hidden.reshape(groups * SUB, tok)

    own_groups = CHUNKS * 2
    for load in loads[:4]:
        load.wait()
    load_x.wait()
    pre = project(w_own, 0, 2, own_groups * 2 * SUB, xv)
    for load in loads[4:]:
        load.wait()
    load_c.wait()
    forward(0)
    grad_hidden = project(w_own, 2, 1, own_groups * SUB, cv)
    both, hidden = hidden_grads(pre, grad_hidden, own_groups)
    term = dot(both, xv[:, theirs], NN)
    own_pair_out[:, :, 0:2] = bf16(term).reshape(CHUNKS, 2, 2, SUB, half)
    term = dot(hidden, cv[:, theirs], NN)
    own_pair_out[:, :, 2:3] = bf16(term).reshape(CHUNKS, 2, 1, SUB, half)
    own_pair = go(remote(own_pair_out, own_pair_in, own_pair_send, own_pair_recv, sibling))
    term = dot(both, xv[:, mine], NN)
    own_sum[:, :, 0:2] = term.reshape(CHUNKS, 2, 2, SUB, half)
    term = dot(hidden, cv[:, mine], NN)
    own_sum[:, :, 2:3] = term.reshape(CHUNKS, 2, 1, SUB, half)
    forward_relayed(0)
    forward(1)

    own_pair.wait_recv()
    across_own = {}
    for k in ACROSS_FIRST:
        own_sum[k] = own_sum[k] + f32(own_pair_in[k])
        across_out[k] = bf16(own_sum[k, 1 - chip])
        across_own[k] = go(
            remote(across_out.at[k], across_own_in.at[k], across_send.at[k], across_recv.at[k], across)
        )
    for k in BACK_FIRST:
        own_sum[k] = own_sum[k] + f32(own_pair_in[k])

    back, across_in = {}, {}

    def later(k):
        arrived(k, 0)
        arrived(k, 1)
        pre = project(w_in.at[k], 0, 2, 4 * SUB, xv)
        arrived(k, 2)
        grad_hidden = project(w_in.at[k], 2, 1, 2 * SUB, cv)
        both, hidden = hidden_grads(pre, grad_hidden, 2)
        term = dot(both, xv[:, theirs], NN)
        in_pair_out[k, :, 0:2] = bf16(term).reshape(2, 2, SUB, half)
        term = dot(hidden, cv[:, theirs], NN)
        in_pair_out[k, :, 2:3] = bf16(term).reshape(2, 1, SUB, half)
        pair = go(remote(in_pair_out.at[k], in_pair_in.at[k], in_pair_send.at[k], in_pair_recv.at[k], sibling))
        term = dot(both, xv[:, mine], NN)
        in_sum[:, 0:2] = term.reshape(2, 2, SUB, half)
        term = dot(hidden, cv[:, mine], NN)
        in_sum[:, 2:3] = term.reshape(2, 1, SUB, half)
        pair.wait_recv()
        if k in BACK_FIRST:
            back_out[k] = bf16(in_sum[...] + f32(in_pair_in[k]))
            back[k] = go(remote(back_out.at[k], back_in.at[k], back_send.at[k], back_recv.at[k], down))
        else:
            other = 1 - down_chip
            across_in_out[k] = bf16(in_sum[other] + f32(in_pair_in[k, other]))
            across_in[k] = go(
                remote(across_in_out.at[k], across_in_in.at[k], across_in_send.at[k], across_in_recv.at[k], across)
            )
            in_keep[k] = in_sum[down_chip] + f32(in_pair_in[k, down_chip])

    in_keep = {}

    def section_sum(k):
        across_in[k].wait_recv()
        back_out[k, 0] = bf16(in_keep[k] + f32(across_in_in[k]))
        back[k] = go(remote(back_out.at[k, 0], back_in.at[k, 0], back_send.at[k], back_recv.at[k], down))

    def merge(k):
        back[k].wait_recv()
        across_out[k] = bf16(own_sum[k, 1 - chip] + f32(back_in[k, 1 - chip]))
        across_own[k] = go(
            remote(across_out.at[k], across_own_in.at[k], across_send.at[k], across_recv.at[k], across)
        )

    def finish(k):
        across_own[k].wait_recv()
        if k in BACK_FIRST:
            returned = back_in[k, chip]
        else:
            back[k].wait_recv()
            returned = back_in[k, 0]
        final[k] = bf16(own_sum[k, chip] + f32(returned) + f32(across_own_in[k]))
        owner = k // 2
        place = out_hbm.at[k % 2, :, :, mine]
        away = remote(final.at[k], place, fin_send.at[k], fin_recv.at[k], sibling)
        here = pltpu.make_async_copy(final.at[k], place, fin_send.at[k])

        @pl.when(core == owner)
        def _():
            here.start()

        @pl.when(core != owner)
        def _():
            away.start()

        def drain():
            @pl.when(core == owner)
            def _():
                here.wait()
                away.wait_recv()

            @pl.when(core != owner)
            def _():
                away.wait_send()

        return drain

    later(0)
    forward_relayed(1)
    later(1)
    forward(2)
    later(2)
    merge(0)
    section_sum(2)
    forward(3)
    later(3)
    merge(1)
    section_sum(3)
    drains = [finish(k) for k in (2, 0, 1, 3)]
    for copy in pending:
        copy.wait_send()
    for drain in drains:
        drain()


def per_device(n_blk, tokens, cotangent, gate_weight, up_weight, down_weight):
    tok, d = tokens.shape
    half = d // 2

    def cut(w):
        return w.reshape(2, CHUNKS, SUB, d)

    hbm = pl.BlockSpec(memory_space=pl.ANY)
    full = (CHUNKS, 2, 3, SUB, d)
    pair = (CHUNKS, 2, 3, SUB, half)
    one = (CHUNKS, 3, SUB, half)
    bf, fl = jnp.bfloat16, jnp.float32
    dma = pltpu.SemaphoreType.DMA
    out = pl.pallas_call(
        functools.partial(kernel, n_blk),
        out_shape=jax.ShapeDtypeStruct((2, 3, SUB, d), bf),
        in_specs=[hbm] * 5,
        out_specs=hbm,
        scratch_shapes=[
            pltpu.VMEM((tok, d), bf), pltpu.VMEM((tok, d), bf), pltpu.VMEM(full, bf), pltpu.VMEM(full, bf),
            pltpu.VMEM(pair, bf), pltpu.VMEM(pair, bf), pltpu.VMEM(pair, fl),
            pltpu.VMEM(pair, bf), pltpu.VMEM(pair, bf), pltpu.VMEM(pair[1:], fl),
            pltpu.VMEM(pair, bf), pltpu.VMEM(pair, bf),
            pltpu.VMEM(one, bf), pltpu.VMEM(one, bf), pltpu.VMEM(one, bf), pltpu.VMEM(one, bf), pltpu.VMEM(one, bf),
            dma((8,)),
            dma((CHUNKS, 3)), dma((CHUNKS, 3)), dma((CHUNKS, 3)), dma((CHUNKS, 3)),
            dma((CHUNKS, 3)), dma((CHUNKS, 3)), dma((CHUNKS, 3)), dma((CHUNKS, 3)),
            dma, dma, dma((CHUNKS,)), dma((CHUNKS,)),
            dma((CHUNKS,)), dma((CHUNKS,)), dma((CHUNKS,)), dma((CHUNKS,)),
            dma((CHUNKS,)), dma((CHUNKS,)), dma((CHUNKS,)), dma((CHUNKS,)),
        ],
        name="window",
        compiler_params=pltpu.CompilerParams(
            collective_id=0, has_side_effects=True, vmem_limit_bytes=58 << 20
        ),
    )(tokens, cotangent, cut(gate_weight), cut(up_weight), cut(down_weight))
    return tuple(out[:, m].reshape(2 * SUB, d) for m in range(3))


def solution(mesh):
    in_specs = (
        P(("blk", "dp"), None),
        P(("blk", "dp"), None),
        P("blk", None),
        P("blk", None),
        P("blk", None),
    )
    out_specs = (P(("blk", "dp"), None),) * 3
    return jax.shard_map(
        functools.partial(per_device, mesh.shape["blk"]),
        mesh=mesh, in_specs=in_specs, out_specs=out_specs, check_vma=False,
    )
```

time: 416 us -> 80.4 us (0.19)
  waiting for transfers between devices: 233 us -> 0 us
  blocking collectives: 140 us -> 0 us
  Pallas kernels: 0 us -> 77.5 us
  matrix products: 28.9 us -> 0 us
  starting transfers between devices: 8.49 us -> 0 us
    ppermute x6 -> x0, waiting for transfers between devices: 233 us -> none  [from_behind(): lax.ppermute(shard, axis, [(i, (i + by) % length) for i in range(length)])]
    psum x1 -> x0, blocking collectives: 140 us -> none  [per_device(): summed = lax.psum((cycle_gate, cycle_up, cycle_down), 'dp')]
    pallas_call x0 -> x1, Pallas kernels: none -> 77.5 us  [per_device(): pl.pallas_call(functools.partial(kernel, n_blk), out_shape=jax.ShapeDtype...]
    dot_general x12 -> x0, matrix products: 28.9 us -> none  [the longest x2 7.17 us: block_terms(): jnp.dot(group_tokens, w_gate.T, preferred_element_type=jnp.float32)]
    ppermute x6 -> x0, starting transfers between devices: 8.49 us -> none  [from_behind(): lax.ppermute(shard, axis, [(i, (i + by) % length) for i in range(length)])]
  transfers between devices with their start and end apart: 6 -> 0, of which waited for: 6 -> 0; matrix products, arithmetic and copies ran while one was open for 5% -> 0% of each run, Pallas kernels for 0% -> 0%
where the time goes in v1:
time: 80.4 us; the launch traced here: 80.2 us
  Pallas kernels  77.5 us (96%)
  local copies, waits for them, and re-layouts  2.14 us (3%)
    pallas_call x1, Pallas kernels, per_device(): pl.pallas_call(functools.partial(kernel, n_blk), out_shape=jax.ShapeDtype...  77.5 us
    slice x1, local copies, waits for them, and re-layouts, per_device(): return tuple((out[:, m].reshape(2 * SUB, d) for m in range(3)))  2.14 us

profile of v1, /device:TPU:1, one launch (start us, length us, event | category | flops | bytes accessed | tf_op | source)
XLA Modules:
  0.0 80.2 jit_solution(2309640672871752656)
XLA Ops:
  0.6 77.5 %window.1 = bf16[2,3,16,5120]{3,2,1,0:T(8,128)(2,1)} custom-call(bf16[384,5120]{1,0:T(8,128)(2,1)} %x_hbm.1, bf16[384,5120]{1,0:T(8,128)(2,1)} %c_hbm.1, bf16[2,4,16,5120]{3,2,1,0:T(8,128)(2,1)} %bitcast.6, bf16[2,4,16,5120]{3,2,1,0:T(8,128)(2,1)} %bitcast.7, bf16[2,4,16,5120]{3,2,1,0:T(8,128)(2,1)} %bitcast.8), custom_call_target="tpu_custom_call" | custom-call | tf_op jit(solution)/shard_map/window/pallas_call | solution.py:287
  78.1 2.1 %fusion = (bf16[2,1,16,5120]{3,2,1,0:T(8,128)(2,1)}, bf16[2,1,16,5120]{3,2,1,0:T(8,128)(2,1)}, bf16[2,1,16,5120]{3,2,1,0:T(8,128)(2,1)}) fusion(bf16[2,3,16,5120]{3,2,1,0:T(8,128)(2,1)} %window.1), kind=kLoop, calls=%fused_computation | loop fusion | bytes 1966080 | tf_op jit(solution)/shard_map/slice | solution.py:310

commit v2 on v1

--- a/solution.py
+++ b/solution.py
@@ -17,6 +17,7 @@
 DIRECT = (2, 3)
 BACK_FIRST = (0, 1)
 ACROSS_FIRST = (2, 3)
+PIECES = (pl.ds(0, 1), pl.ds(1, 1), pl.ds(2, 1))
 
 
 def dot(a, b, dims):
@@ -100,21 +101,19 @@
 
     fwd, relay, fwd2 = {}, {}, {}
 
-    def forward(k):
-        for m in range(3):
-            up_copies[k, m].wait_recv()
-            if k in RELAY:
-                piece = w_in.at[k, chip, m, :, mine]
-                relay[k, m] = go(remote(piece, piece, relay_send.at[k, m], relay_recv.at[k, m], across))
-            else:
-                piece = w_in.at[k, :, m, :, mine]
-            fwd[k, m] = go(remote(piece, piece, fwd_send.at[k, m], fwd_recv.at[k, m], sibling))
-
-    def forward_relayed(k):
-        for m in range(3):
-            relay[k, m].wait_recv()
-            piece = w_in.at[k, 1 - chip, m, :, mine]
-            fwd2[k, m] = go(remote(piece, piece, fwd2_send.at[k, m], fwd2_recv.at[k, m], sibling))
+    def forward(k, m):
+        up_copies[k, m].wait_recv()
+        if k in RELAY:
+            piece = w_in.at[k, chip, m, :, mine]
+            relay[k, m] = go(remote(piece, piece, relay_send.at[k, m], relay_recv.at[k, m], across))
+        else:
+            piece = w_in.at[k, :, m, :, mine]
+        fwd[k, m] = go(remote(piece, piece, fwd_send.at[k, m], fwd_recv.at[k, m], sibling))
+
+    def forward_relayed(k, m):
+        relay[k, m].wait_recv()
+        piece = w_in.at[k, 1 - chip, m, :, mine]
+        fwd2[k, m] = go(remote(piece, piece, fwd2_send.at[k, m], fwd2_recv.at[k, m], sibling))
 
     def arrived(k, m):
         fwd[k, m].wait_recv()
@@ -129,109 +128,141 @@
             total = term if total is None else total + term
         return total
 
-    def hidden_grads(pre, grad_hidden, groups):
+    def forward_parts(pre, groups):
         tok = pre.shape[-1]
         pre = pre.reshape(groups, 2, SUB, tok)
         gate, up_pre = pre[:, 0], pre[:, 1]
-        grad_hidden = grad_hidden.reshape(groups, SUB, tok)
         squash = jax.nn.sigmoid(gate)
         silu = gate * squash
-        hidden = bf16(silu * up_pre)
-        gg = bf16(grad_hidden * up_pre * squash * (1.0 + gate * (1.0 - squash)))
-        gu = bf16(grad_hidden * silu)
-        both = jnp.stack([gg, gu], axis=1).reshape(groups * 2 * SUB, tok)
-        return both, hidden.reshape(groups * SUB, tok)
+        hidden = bf16(silu * up_pre).reshape(groups * SUB, tok)
+        slope = up_pre * squash * (1.0 + gate * (1.0 - squash))
+        return hidden, slope, silu
+
+    def backward_parts(grad_hidden, slope, silu, groups):
+        tok = grad_hidden.shape[-1]
+        grad_hidden = grad_hidden.reshape(groups, SUB, tok)
+        both = jnp.stack([bf16(grad_hidden * slope), bf16(grad_hidden * silu)], axis=1)
+        return both.reshape(groups * 2 * SUB, tok)
 
     own_groups = CHUNKS * 2
     for load in loads[:4]:
         load.wait()
     load_x.wait()
     pre = project(w_own, 0, 2, own_groups * 2 * SUB, xv)
+    forward(0, 0)
     for load in loads[4:]:
         load.wait()
     load_c.wait()
-    forward(0)
     grad_hidden = project(w_own, 2, 1, own_groups * SUB, cv)
-    both, hidden = hidden_grads(pre, grad_hidden, own_groups)
+    forward(0, 1)
+    hidden, slope, silu = forward_parts(pre, own_groups)
+    both = backward_parts(grad_hidden, slope, silu, own_groups)
     term = dot(both, xv[:, theirs], NN)
     own_pair_out[:, :, 0:2] = bf16(term).reshape(CHUNKS, 2, 2, SUB, half)
     term = dot(hidden, cv[:, theirs], NN)
     own_pair_out[:, :, 2:3] = bf16(term).reshape(CHUNKS, 2, 1, SUB, half)
-    own_pair = go(remote(own_pair_out, own_pair_in, own_pair_send, own_pair_recv, sibling))
+    own_pair = {}
+    for g, ks in enumerate((ACROSS_FIRST, BACK_FIRST)):
+        s = pl.ds(ks[0], len(ks))
+        own_pair[g] = go(
+            remote(own_pair_out.at[s], own_pair_in.at[s], own_pair_send.at[g], own_pair_recv.at[g], sibling)
+        )
+    forward(0, 2)
     term = dot(both, xv[:, mine], NN)
     own_sum[:, :, 0:2] = term.reshape(CHUNKS, 2, 2, SUB, half)
+    forward_relayed(0, 0)
+    forward_relayed(0, 1)
     term = dot(hidden, cv[:, mine], NN)
     own_sum[:, :, 2:3] = term.reshape(CHUNKS, 2, 1, SUB, half)
-    forward_relayed(0)
-    forward(1)
-
-    own_pair.wait_recv()
-    across_own = {}
-    for k in ACROSS_FIRST:
-        own_sum[k] = own_sum[k] + f32(own_pair_in[k])
+    forward_relayed(0, 2)
+    forward(1, 0)
+
+    across_own, across_in, back, pair, state = {}, {}, {}, {}, {}
+
+    def own_chip_sums(g, ks):
+        own_pair[g].wait_recv()
+        for k in ks:
+            own_sum[k] = own_sum[k] + f32(own_pair_in[k])
+
+    def send_own(k):
         across_out[k] = bf16(own_sum[k, 1 - chip])
         across_own[k] = go(
             remote(across_out.at[k], across_own_in.at[k], across_send.at[k], across_recv.at[k], across)
         )
-    for k in BACK_FIRST:
-        own_sum[k] = own_sum[k] + f32(own_pair_in[k])
-
-    back, across_in = {}, {}
-
-    def later(k):
+
+    def pair_send(k, n, s):
+        pair[k, n] = go(
+            remote(
+                in_pair_out.at[k, :, s], in_pair_in.at[k, :, s], in_pair_send.at[k, n], in_pair_recv.at[k, n], sibling
+            )
+        )
+
+    def down_terms(k):
         arrived(k, 0)
         arrived(k, 1)
         pre = project(w_in.at[k], 0, 2, 4 * SUB, xv)
-        arrived(k, 2)
-        grad_hidden = project(w_in.at[k], 2, 1, 2 * SUB, cv)
-        both, hidden = hidden_grads(pre, grad_hidden, 2)
-        term = dot(both, xv[:, theirs], NN)
-        in_pair_out[k, :, 0:2] = bf16(term).reshape(2, 2, SUB, half)
+        hidden, slope, silu = forward_parts(pre, 2)
         term = dot(hidden, cv[:, theirs], NN)
         in_pair_out[k, :, 2:3] = bf16(term).reshape(2, 1, SUB, half)
-        pair = go(remote(in_pair_out.at[k], in_pair_in.at[k], in_pair_send.at[k], in_pair_recv.at[k], sibling))
-        term = dot(both, xv[:, mine], NN)
-        in_sum[:, 0:2] = term.reshape(2, 2, SUB, half)
+        pair_send(k, 1, pl.ds(2, 1))
         term = dot(hidden, cv[:, mine], NN)
-        in_sum[:, 2:3] = term.reshape(2, 1, SUB, half)
-        pair.wait_recv()
-        if k in BACK_FIRST:
-            back_out[k] = bf16(in_sum[...] + f32(in_pair_in[k]))
-            back[k] = go(remote(back_out.at[k], back_in.at[k], back_send.at[k], back_recv.at[k], down))
-        else:
-            other = 1 - down_chip
-            across_in_out[k] = bf16(in_sum[other] + f32(in_pair_in[k, other]))
-            across_in[k] = go(
-                remote(across_in_out.at[k], across_in_in.at[k], across_in_send.at[k], across_in_recv.at[k], across)
+        in_sum[k, :, 2:3] = term.reshape(2, 1, SUB, half)
+        state[k] = slope, silu
+
+    def back_project(k):
+        arrived(k, 2)
+        state[k] = backward_parts(project(w_in.at[k], 2, 1, 2 * SUB, cv), *state[k], 2)
+
+    def gate_up_theirs(k):
+        term = dot(state[k], xv[:, theirs], NN)
+        in_pair_out[k, :, 0:2] = bf16(term).reshape(2, 2, SUB, half)
+        pair_send(k, 0, pl.ds(0, 2))
+
+    def gate_up_mine(k):
+        term = dot(state[k], xv[:, mine], NN)
+        in_sum[k, :, 0:2] = term.reshape(2, 2, SUB, half)
+
+    def send_back(k):
+        pair[k, 0].wait_recv()
+        pair[k, 1].wait_recv()
+        back_out[k] = bf16(in_sum[k] + f32(in_pair_in[k]))
+        back[k, 0] = go(remote(back_out.at[k], back_in.at[k], back_send.at[k, 0], back_recv.at[k, 0], down))
+
+    def send_across(k, n):
+        if n != 1:
+            pair[k, n // 2].wait_recv()
+        s = PIECES[n]
+        other = 1 - down_chip
+        across_in_out[k, s] = bf16(in_sum[k, other, s] + f32(in_pair_in[k, other, s]))
+        across_in[k, n] = go(
+            remote(
+                across_in_out.at[k, s], across_in_in.at[k, s], across_in_send.at[k, n], across_in_recv.at[k, n], across
             )
-            in_keep[k] = in_sum[down_chip] + f32(in_pair_in[k, down_chip])
-
-    in_keep = {}
-
-    def section_sum(k):
-        across_in[k].wait_recv()
-        back_out[k, 0] = bf16(in_keep[k] + f32(across_in_in[k]))
-        back[k] = go(remote(back_out.at[k, 0], back_in.at[k, 0], back_send.at[k], back_recv.at[k], down))
+        )
+
+    def section_sum(k, n):
+        across_in[k, n].wait_recv()
+        s = PIECES[n]
+        total = in_sum[k, down_chip, s] + f32(in_pair_in[k, down_chip, s]) + f32(across_in_in[k, s])
+        back_out[k, 0, s] = bf16(total)
+        back[k, n] = go(
+            remote(back_out.at[k, 0, s], back_in.at[k, 0, s], back_send.at[k, n], back_recv.at[k, n], down)
+        )
 
     def merge(k):
-        back[k].wait_recv()
+        back[k, 0].wait_recv()
         across_out[k] = bf16(own_sum[k, 1 - chip] + f32(back_in[k, 1 - chip]))
         across_own[k] = go(
             remote(across_out.at[k], across_own_in.at[k], across_send.at[k], across_recv.at[k], across)
         )
 
-    def finish(k):
-        across_own[k].wait_recv()
-        if k in BACK_FIRST:
-            returned = back_in[k, chip]
-        else:
-            back[k].wait_recv()
-            returned = back_in[k, 0]
-        final[k] = bf16(own_sum[k, chip] + f32(returned) + f32(across_own_in[k]))
+    drains = []
+
+    def write(k, n, s):
         owner = k // 2
-        place = out_hbm.at[k % 2, :, :, mine]
-        away = remote(final.at[k], place, fin_send.at[k], fin_recv.at[k], sibling)
-        here = pltpu.make_async_copy(final.at[k], place, fin_send.at[k])
+        place = out_hbm.at[k % 2, s, :, mine]
+        away = remote(final.at[k, s], place, fin_send.at[k, n], fin_recv.at[k, n], sibling)
+        here = pltpu.make_async_copy(final.at[k, s], place, fin_send.at[k, n])
 
         @pl.when(core == owner)
         def _():
@@ -251,20 +282,71 @@
             def _():
                 away.wait_send()
 
-        return drain
-
-    later(0)
-    forward_relayed(1)
-    later(1)
-    forward(2)
-    later(2)
+        drains.append(drain)
+
+    def finish_back(k):
+        across_own[k].wait_recv()
+        final[k] = bf16(own_sum[k, chip] + f32(back_in[k, chip]) + f32(across_own_in[k]))
+        write(k, 0, pl.ds(0, 3))
+
+    def finish_across(k, n):
+        if n == 2:
+            across_own[k].wait_recv()
+        back[k, n].wait_recv()
+        s = PIECES[n]
+        final[k, s] = bf16(own_sum[k, chip, s] + f32(back_in[k, 0, s]) + f32(across_own_in[k, s]))
+        write(k, n, s)
+
+    own_chip_sums(0, ACROSS_FIRST)
+    down_terms(0)
+    forward(1, 1)
+    back_project(0)
+    forward(1, 2)
+    send_own(2)
+    send_own(3)
+    gate_up_theirs(0)
+    forward_relayed(1, 0)
+    forward_relayed(1, 1)
+    gate_up_mine(0)
+    forward_relayed(1, 2)
+    own_chip_sums(1, BACK_FIRST)
+    send_back(0)
+    down_terms(1)
+    back_project(1)
+    gate_up_theirs(1)
+    forward(2, 0)
+    gate_up_mine(1)
+    forward(2, 1)
+    send_back(1)
+    forward(2, 2)
+    down_terms(2)
+    back_project(2)
+    gate_up_theirs(2)
+    gate_up_mine(2)
+    forward(3, 0)
+    for n in (2, 0, 1):
+        send_across(2, n)
+    forward(3, 1)
+    down_terms(3)
     merge(0)
-    section_sum(2)
-    forward(3)
-    later(3)
+    forward(3, 2)
+    send_across(3, 2)
+    back_project(3)
+    gate_up_theirs(3)
+    gate_up_mine(3)
+    for n in (0, 1):
+        send_across(3, n)
+    for n in (2, 0, 1):
+        section_sum(2, n)
     merge(1)
-    section_sum(3)
-    drains = [finish(k) for k in (2, 0, 1, 3)]
+    for n in (2, 0, 1):
+        section_sum(3, n)
+    finish_back(0)
+    for n in (2, 0, 1):
+        finish_across(2, n)
+    for n in (2, 0, 1):
+        finish_across(3, n)
+    finish_back(1)
     for copy in pending:
         copy.wait_send()
     for drain in drains:
@@ -292,15 +374,15 @@
         scratch_shapes=[
             pltpu.VMEM((tok, d), bf), pltpu.VMEM((tok, d), bf), pltpu.VMEM(full, bf), pltpu.VMEM(full, bf),
             pltpu.VMEM(pair, bf), pltpu.VMEM(pair, bf), pltpu.VMEM(pair, fl),
-            pltpu.VMEM(pair, bf), pltpu.VMEM(pair, bf), pltpu.VMEM(pair[1:], fl),
+            pltpu.VMEM(pair, bf), pltpu.VMEM(pair, bf), pltpu.VMEM(pair, fl),
             pltpu.VMEM(pair, bf), pltpu.VMEM(pair, bf),
             pltpu.VMEM(one, bf), pltpu.VMEM(one, bf), pltpu.VMEM(one, bf), pltpu.VMEM(one, bf), pltpu.VMEM(one, bf),
             dma((8,)),
             dma((CHUNKS, 3)), dma((CHUNKS, 3)), dma((CHUNKS, 3)), dma((CHUNKS, 3)),
             dma((CHUNKS, 3)), dma((CHUNKS, 3)), dma((CHUNKS, 3)), dma((CHUNKS, 3)),
-            dma, dma, dma((CHUNKS,)), dma((CHUNKS,)),
-            dma((CHUNKS,)), dma((CHUNKS,)), dma((CHUNKS,)), dma((CHUNKS,)),
-            dma((CHUNKS,)), dma((CHUNKS,)), dma((CHUNKS,)), dma((CHUNKS,)),
+            dma((2,)), dma((2,)), dma((CHUNKS, 2)), dma((CHUNKS, 2)),
+            dma((CHUNKS, 3)), dma((CHUNKS, 3)), dma((CHUNKS, 3)), dma((CHUNKS, 3)),
+            dma((CHUNKS,)), dma((CHUNKS,)), dma((CHUNKS, 3)), dma((CHUNKS, 3)),
         ],
         name="window",
         compiler_params=pltpu.CompilerParams(

time: 80.4 us -> 72.8 us (0.905)
  Pallas kernels: 77.5 us -> 69.9 us
    pallas_call x1, Pallas kernels: 77.5 us -> 69.9 us  [per_device(): pl.pallas_call(functools.partial(kernel, n_blk), out_shape=jax.ShapeDtype...]
where the time goes in v2:
time: 72.8 us; the launch traced here: 72.7 us
  Pallas kernels  69.9 us (96%)
  local copies, waits for them, and re-layouts  2.14 us (3%)
    pallas_call x1, Pallas kernels, per_device(): pl.pallas_call(functools.partial(kernel, n_blk), out_shape=jax.ShapeDtype...  69.9 us
    slice x1, local copies, waits for them, and re-layouts, per_device(): return tuple((out[:, m].reshape(2 * SUB, d) for m in range(3)))  2.14 us

profile of v2, /device:TPU:1, one launch (start us, length us, event | category | flops | bytes accessed | tf_op | source)
XLA Modules:
  0.0 72.7 jit_solution(17389700476856173902)
XLA Ops:
  0.6 69.9 %window.1 = bf16[2,3,16,5120]{3,2,1,0:T(8,128)(2,1)} custom-call(bf16[384,5120]{1,0:T(8,128)(2,1)} %x_hbm.1, bf16[384,5120]{1,0:T(8,128)(2,1)} %c_hbm.1, bf16[2,4,16,5120]{3,2,1,0:T(8,128)(2,1)} %bitcast.6, bf16[2,4,16,5120]{3,2,1,0:T(8,128)(2,1)} %bitcast.7, bf16[2,4,16,5120]{3,2,1,0:T(8,128)(2,1)} %bitcast.8), custom_call_target="tpu_custom_call" | custom-call | tf_op jit(solution)/shard_map/window/pallas_call | solution.py:369
  70.5 2.1 %fusion = (bf16[2,1,16,5120]{3,2,1,0:T(8,128)(2,1)}, bf16[2,1,16,5120]{3,2,1,0:T(8,128)(2,1)}, bf16[2,1,16,5120]{3,2,1,0:T(8,128)(2,1)}) fusion(bf16[2,3,16,5120]{3,2,1,0:T(8,128)(2,1)} %window.1), kind=kLoop, calls=%fused_computation | loop fusion | bytes 1966080 | tf_op jit(solution)/shard_map/slice | solution.py:392

commit v3 on v2

--- a/solution.py
+++ b/solution.py
@@ -161,12 +161,6 @@
     own_pair_out[:, :, 0:2] = bf16(term).reshape(CHUNKS, 2, 2, SUB, half)
     term = dot(hidden, cv[:, theirs], NN)
     own_pair_out[:, :, 2:3] = bf16(term).reshape(CHUNKS, 2, 1, SUB, half)
-    own_pair = {}
-    for g, ks in enumerate((ACROSS_FIRST, BACK_FIRST)):
-        s = pl.ds(ks[0], len(ks))
-        own_pair[g] = go(
-            remote(own_pair_out.at[s], own_pair_in.at[s], own_pair_send.at[g], own_pair_recv.at[g], sibling)
-        )
     forward(0, 2)
     term = dot(both, xv[:, mine], NN)
     own_sum[:, :, 0:2] = term.reshape(CHUNKS, 2, 2, SUB, half)
@@ -175,7 +169,14 @@
     term = dot(hidden, cv[:, mine], NN)
     own_sum[:, :, 2:3] = term.reshape(CHUNKS, 2, 1, SUB, half)
     forward_relayed(0, 2)
+    own_pair = {}
+    for g, ks in enumerate((ACROSS_FIRST, BACK_FIRST)):
+        s = pl.ds(ks[0], len(ks))
+        own_pair[g] = go(
+            remote(own_pair_out.at[s], own_pair_in.at[s], own_pair_send.at[g], own_pair_recv.at[g], sibling)
+        )
     forward(1, 0)
+    forward(1, 1)
 
     across_own, across_in, back, pair, state = {}, {}, {}, {}, {}
 
@@ -260,7 +261,7 @@
 
     def write(k, n, s):
         owner = k // 2
-        place = out_hbm.at[k % 2, s, :, mine]
+        place = out_hbm.at[s, k % 2, :, mine]
         away = remote(final.at[k, s], place, fin_send.at[k, n], fin_recv.at[k, n], sibling)
         here = pltpu.make_async_copy(final.at[k, s], place, fin_send.at[k, n])
 
@@ -297,47 +298,46 @@
         final[k, s] = bf16(own_sum[k, chip, s] + f32(back_in[k, 0, s]) + f32(across_own_in[k, s]))
         write(k, n, s)
 
+    down_terms(0)
+    forward(1, 2)
+    back_project(0)
+    gate_up_theirs(0)
     own_chip_sums(0, ACROSS_FIRST)
-    down_terms(0)
-    forward(1, 1)
-    back_project(0)
-    forward(1, 2)
     send_own(2)
     send_own(3)
-    gate_up_theirs(0)
+    gate_up_mine(0)
     forward_relayed(1, 0)
     forward_relayed(1, 1)
-    gate_up_mine(0)
+    send_back(0)
     forward_relayed(1, 2)
+    forward(2, 0)
     own_chip_sums(1, BACK_FIRST)
-    send_back(0)
     down_terms(1)
+    forward(2, 1)
     back_project(1)
     gate_up_theirs(1)
-    forward(2, 0)
+    forward(2, 2)
     gate_up_mine(1)
-    forward(2, 1)
     send_back(1)
-    forward(2, 2)
     down_terms(2)
     back_project(2)
     gate_up_theirs(2)
+    forward(3, 0)
     gate_up_mine(2)
-    forward(3, 0)
     for n in (2, 0, 1):
         send_across(2, n)
+    merge(0)
     forward(3, 1)
     down_terms(3)
-    merge(0)
     forward(3, 2)
     send_across(3, 2)
     back_project(3)
     gate_up_theirs(3)
+    for n in (2, 0, 1):
+        section_sum(2, n)
     gate_up_mine(3)
     for n in (0, 1):
         send_across(3, n)
-    for n in (2, 0, 1):
-        section_sum(2, n)
     merge(1)
     for n in (2, 0, 1):
         section_sum(3, n)
@@ -368,7 +368,7 @@
     dma = pltpu.SemaphoreType.DMA
     out = pl.pallas_call(
         functools.partial(kernel, n_blk),
-        out_shape=jax.ShapeDtypeStruct((2, 3, SUB, d), bf),
+        out_shape=jax.ShapeDtypeStruct((3, 2, SUB, d), bf),
         in_specs=[hbm] * 5,
         out_specs=hbm,
         scratch_shapes=[
@@ -389,7 +389,7 @@
             collective_id=0, has_side_effects=True, vmem_limit_bytes=58 << 20
         ),
     )(tokens, cotangent, cut(gate_weight), cut(up_weight), cut(down_weight))
-    return tuple(out[:, m].reshape(2 * SUB, d) for m in range(3))
+    return tuple(out[m].reshape(2 * SUB, d) for m in range(3))
 
 
 def solution(mesh):

time: 72.8 us -> 71 us (0.975)
  Pallas kernels: 69.9 us -> 68.2 us
    pallas_call x1, Pallas kernels: 69.9 us -> 68.2 us  [per_device(): pl.pallas_call(functools.partial(kernel, n_blk), out_shape=jax.ShapeDtype...]
where the time goes in v3:
time: 71 us; the launch traced here: 70.9 us
  Pallas kernels  68.2 us (96%)
  local copies, waits for them, and re-layouts  2.13 us (3%)
    pallas_call x1, Pallas kernels, per_device(): pl.pallas_call(functools.partial(kernel, n_blk), out_shape=jax.ShapeDtype...  68.2 us
    slice x1, local copies, waits for them, and re-layouts, per_device(): return tuple((out[m].reshape(2 * SUB, d) for m in range(3)))  2.13 us

profile of v3, /device:TPU:1, one launch (start us, length us, event | category | flops | bytes accessed | tf_op | source)
XLA Modules:
  0.0 70.9 jit_solution(10352159436171762202)
XLA Ops:
  0.6 68.2 %window.1 = bf16[3,2,16,5120]{3,2,1,0:T(8,128)(2,1)} custom-call(bf16[384,5120]{1,0:T(8,128)(2,1)} %x_hbm.1, bf16[384,5120]{1,0:T(8,128)(2,1)} %c_hbm.1, bf16[2,4,16,5120]{3,2,1,0:T(8,128)(2,1)} %bitcast.6, bf16[2,4,16,5120]{3,2,1,0:T(8,128)(2,1)} %bitcast.7, bf16[2,4,16,5120]{3,2,1,0:T(8,128)(2,1)} %bitcast.8), custom_call_target="tpu_custom_call" | custom-call | tf_op jit(solution)/shard_map/window/pallas_call | solution.py:369
  68.8 2.1 %fusion = (bf16[1,2,16,5120]{3,2,1,0:T(8,128)(2,1)}, bf16[1,2,16,5120]{3,2,1,0:T(8,128)(2,1)}, bf16[1,2,16,5120]{3,2,1,0:T(8,128)(2,1)}) fusion(bf16[3,2,16,5120]{3,2,1,0:T(8,128)(2,1)} %window.1), kind=kLoop, calls=%fused_computation | loop fusion | bytes 1966080 | tf_op jit(solution)/shard_map/slice | solution.py:392

commit v4 on v3

--- a/solution.py
+++ b/solution.py
@@ -339,9 +339,10 @@
     for n in (0, 1):
         send_across(3, n)
     merge(1)
-    for n in (2, 0, 1):
+    section_sum(3, 2)
+    finish_back(0)
+    for n in (0, 1):
         section_sum(3, n)
-    finish_back(0)
     for n in (2, 0, 1):
         finish_across(2, n)
     for n in (2, 0, 1):

time: 71 us -> 71 us (level)
  no operation moved by 1% of the time
where the time goes in v4:
time: 71 us; the launch traced here: 70.9 us
  Pallas kernels  68.2 us (96%)
  local copies, waits for them, and re-layouts  2.13 us (3%)
    pallas_call x1, Pallas kernels, per_device(): pl.pallas_call(functools.partial(kernel, n_blk), out_shape=jax.ShapeDtype...  68.2 us
    slice x1, local copies, waits for them, and re-layouts, per_device(): return tuple((out[m].reshape(2 * SUB, d) for m in range(3)))  2.13 us

profile of v4, /device:TPU:1, one launch (start us, length us, event | category | flops | bytes accessed | tf_op | source)
XLA Modules:
  0.0 70.9 jit_solution(16671458625966056477)
XLA Ops:
  0.6 68.2 %window.1 = bf16[3,2,16,5120]{3,2,1,0:T(8,128)(2,1)} custom-call(bf16[384,5120]{1,0:T(8,128)(2,1)} %x_hbm.1, bf16[384,5120]{1,0:T(8,128)(2,1)} %c_hbm.1, bf16[2,4,16,5120]{3,2,1,0:T(8,128)(2,1)} %bitcast.6, bf16[2,4,16,5120]{3,2,1,0:T(8,128)(2,1)} %bitcast.7, bf16[2,4,16,5120]{3,2,1,0:T(8,128)(2,1)} %bitcast.8), custom_call_target="tpu_custom_call" | custom-call | tf_op jit(solution)/shard_map/window/pallas_call | solution.py:370
  68.8 2.1 %fusion = (bf16[1,2,16,5120]{3,2,1,0:T(8,128)(2,1)}, bf16[1,2,16,5120]{3,2,1,0:T(8,128)(2,1)}, bf16[1,2,16,5120]{3,2,1,0:T(8,128)(2,1)}) fusion(bf16[3,2,16,5120]{3,2,1,0:T(8,128)(2,1)} %window.1), kind=kLoop, calls=%fused_computation | loop fusion | bytes 1966080 | tf_op jit(solution)/shard_map/slice | solution.py:393
